TPU v7x, 256 devices: a whole 4x4x8 slice. The times are simulated.
256 devices in a mesh: pb: 32 (over z, x), ha: 8 (over y, core).
Axes of the slice: x: 4, y: 4, z: 8, core: 2. Of those that a mesh axis runs over, the one named last changes fastest.
Arguments:
- queries: bfloat16 [4096, 4096], P('pb', 'ha')
- keys: bfloat16 [4096, 4096], P('pb', 'ha')
- values: bfloat16 [4096, 4096], P('pb', 'ha'), may hold values from -6 to 6
- theta: float32 [32, 6, 11], P('ha')
- mix: float32 [32, 4], P('ha')
- gain: float32 [4096], P('ha'), may hold values from 0.5 to 1.5
- out_weight: bfloat16 [4096, 4096], P('ha'), may hold values from -0.09375 to 0.09375
- turn_lengths: int32 [16], replicated, may hold values from 1 to 640, 4096 in all
Outputs:
- output: bfloat16 [4096, 4096], P('pb', 'ha')
Inputs may be any that keep to these rules, and one draw needn't show every extreme that they name: `turn_lengths`: the turns' lengths sum to 4096; the longest turn has exactly 640 positions.
All inputs are finite; a program needn't handle non-finite values.
Results may differ from a plain program's by a relative error of at most 0.018.
Values may be sent and summed in bfloat16 or wider, within the bound.
A program may use at most 64 MiB of HBM per device.

v0:
```python
import functools
import math

import jax
import jax.numpy as jnp
from jax import lax
from jax.experimental import pallas as pl
from jax.experimental.pallas import tpu as pltpu
from jax.sharding import PartitionSpec as P

GROUP = 4
QCONV = 6
KCONV = 11
REACH = (KCONV - 1) // 2
MAXBACK = 5
ROWS = 128
DH = 128
COLS = GROUP * DH
RING_X = 4
CORES = 2
PAD = 16
STEP = 112
WINDOWS = 7
SPAN = PAD + (MAXBACK + 1) * ROWS + PAD
QROWS = PAD + ROWS
HALF = ROWS // 2
MESH = pl.DeviceIdType.MESH
Z_OWN, X_ONE, X_THREE, X_TWO, Z_FIVE = range(5)


def slot_row(distance):
    return PAD + (MAXBACK - distance) * ROWS


def kernel(
    pb_size,
    ha_size,
    turns_ref,
    q_hbm,
    k_hbm,
    v_hbm,
    theta_ref,
    mix_ref,
    gain_ref,
    w_hbm,
    out_ref,
    qext,
    kwin,
    vwin,
    w_vmem,
    taps,
    band,
    row_lo,
    row_hi,
    row_ok,
    shifted,
    lhs,
    conv_buf,
    probs,
    inv_total,
    vext,
    acc,
    normed,
    core_out,
    core_in,
    chip_out,
    chip_in,
    load_sem,
    tail_sem,
    send_sem,
    recv_sem,
    core_send,
    core_recv,
    chip_send,
    chip_recv,
):
    pb = lax.axis_index("pb")
    ha = lax.axis_index("ha")
    ring_z = pb_size // RING_X
    ring_y = ha_size // CORES
    x, z = pb % RING_X, pb // RING_X
    core, y = ha % CORES, ha // CORES

    def at(new_z, new_x):
        return ((new_z % ring_z) * RING_X + new_x % RING_X, ha)

    x_next, x_back = at(z, x + 1), at(z, x + RING_X - 1)
    z_next, z_back = at(z + 1, x), at(z + ring_z - 1, x)
    pb_next, pb_back = ((pb + 1) % pb_size, ha), ((pb + pb_size - 1) % pb_size, ha)
    twin = (pb, y * CORES + 1 - core)

    def chip(k):
        return (pb, ((y + k) % ring_y) * CORES + core)

    own = slot_row(0)
    loads = [
        pltpu.make_async_copy(k_hbm, kwin.at[pl.ds(own, ROWS)], load_sem.at[0]),
        pltpu.make_async_copy(v_hbm, vwin.at[pl.ds(own, ROWS)], load_sem.at[1]),
        pltpu.make_async_copy(q_hbm, qext.at[pl.ds(PAD, ROWS)], load_sem.at[2]),
        pltpu.make_async_copy(w_hbm, w_vmem, load_sem.at[3]),
    ]
    for load in loads:
        load.start()

    barrier = pltpu.get_barrier_semaphore()
    greeted = [x_next, x_back, z_next, z_back, pb_next, pb_back, twin]
    greeted += [chip(k) for k in range(1, ring_y)]
    for other in greeted:
        pl.semaphore_signal(barrier, inc=1, device_id=other, device_id_type=MESH)
    pl.semaphore_wait(barrier, len(greeted))

    def message(kind, chunk):
        win = kwin if chunk < 2 else vwin
        shift = (chunk % 2) * HALF
        last = x == RING_X - 1
        src, dst, target = {
            Z_OWN: (own, slot_row(4), z_next),
            X_ONE: (jnp.where(last, slot_row(4), own), slot_row(1), x_next),
            X_THREE: (jnp.where(x == 0, own, slot_row(4)), slot_row(3), x_back),
            X_TWO: (jnp.where(last, slot_row(5), slot_row(1)), slot_row(2), x_next),
            Z_FIVE: (slot_row(1), slot_row(5), z_next),
        }[kind]
        return pltpu.make_async_remote_copy(
            src_ref=win.at[pl.ds(pl.multiple_of(src + shift, 16), HALF)],
            dst_ref=win.at[pl.ds(dst + shift, HALF)],
            send_sem=send_sem.at[kind, chunk],
            recv_sem=recv_sem.at[kind, chunk],
            device_id=target,
            device_id_type=MESH,
        )

    tail = pltpu.make_async_remote_copy(
        src_ref=qext.at[pl.ds(ROWS, PAD)],
        dst_ref=qext.at[pl.ds(0, PAD)],
        send_sem=tail_sem.at[0],
        recv_sem=tail_sem.at[1],
        device_id=pb_next,
        device_id_type=MESH,
    )

    def first(chunk):
        message(Z_OWN, chunk).start()

        @pl.when(x < RING_X - 1)
        def _():
            message(X_ONE, chunk).start()

        @pl.when(x == 0)
        def _():
            message(X_THREE, chunk).start()

    def after_four(chunk):
        message(Z_OWN, chunk).wait_recv()

        @pl.when(x == RING_X - 1)
        def _():
            message(X_ONE, chunk).start()

        @pl.when(x > 0)
        def _():
            message(X_THREE, chunk).start()

    def after_one(chunk):
        message(X_ONE, chunk).wait_recv()
        message(Z_FIVE, chunk).start()

        @pl.when(x < RING_X - 1)
        def _():
            message(X_TWO, chunk).start()

    def after_five(chunk):
        message(Z_FIVE, chunk).wait_recv()

        @pl.when(x == RING_X - 1)
        def _():
            message(X_TWO, chunk).start()

    def last_two(chunk):
        message(X_TWO, chunk).wait_recv()
        message(X_THREE, chunk).wait_recv()

    loads[0].wait()
    first(0)
    first(1)
    loads[2].wait()
    tail.start()

    first_row = pb * ROWS
    for win in (kwin, vwin):
        win[0:PAD] = jnp.zeros((PAD, COLS), jnp.bfloat16)
        win[SPAN - PAD : SPAN] = jnp.zeros((PAD, COLS), jnp.bfloat16)
    pos = first_row - PAD + lax.broadcasted_iota(jnp.int32, (QROWS, DH), 0)
    row_start = jnp.zeros((QROWS, DH), jnp.int32)
    start = jnp.int32(0)
    for n in range(turns_ref.shape[0]):
        row_start = jnp.where(pos >= start, start, row_start)
        start = start + turns_ref[n]
    key_zero = first_row - slot_row(0)
    row_lo[...] = row_start - key_zero
    row_hi[...] = pos - key_zero
    rel = (pos - row_start)[PAD:]
    for a in range(QCONV):
        row_ok[a] = jnp.where(rel >= a, 1.0, 0.0).astype(jnp.bfloat16)
    taps[...] = jnp.zeros(taps.shape, jnp.float32)
    scaled_theta = theta_ref[...] * (1.0 / math.sqrt(DH))
    taps[:, 0:QCONV, 0 : REACH + 1] = scaled_theta[:, :, REACH:]
    taps[:, 0:QCONV, DH - REACH : DH] = scaled_theta[:, :, :REACH]

    after_four(0)
    after_four(1)
    loads[1].wait()

    def make_band(h, carry):
        for a in range(QCONV):
            line = jnp.broadcast_to(taps[h, a : a + 1, :], (DH, DH))
            square = pltpu.roll(line, 0, 1, stride=1, stride_axis=0)
            band[h, a * DH : (a + 1) * DH, :] = square.astype(jnp.bfloat16)
        return carry

    lax.fori_loop(0, 2, make_band, 0)
    after_one(0)
    after_one(1)
    first(2)
    first(3)
    lax.fori_loop(2, 4, make_band, 0)
    after_five(0)
    after_five(1)
    tail.wait_recv()
    last_two(0)
    last_two(1)

    lane = lax.broadcasted_iota(jnp.int32, (ROWS, DH), 1)
    q_lane = lax.broadcasted_iota(jnp.int32, (QROWS, DH), 1)
    inner = (lane >= 8) & (lane < 8 + STEP)

    def head(h, carry):
        cols = pl.ds(pl.multiple_of(h * DH, DH), DH)
        q_head = qext[:, cols]
        for t in range(WINDOWS):
            k_head = kwin[t * STEP : t * STEP + DH, cols]
            scores = lax.dot_general(
                q_head, k_head, (((1,), (1,)), ((), ())), preferred_element_type=jnp.float32
            )
            place = q_lane + t * STEP
            seen = (place >= row_lo[...]) & (place <= row_hi[...])
            shifted[t] = jnp.where(seen, scores, 0.0)
        for t in range(WINDOWS):
            for a in range(QCONV):
                moved = shifted[t, PAD - a : PAD - a + ROWS, :].astype(jnp.bfloat16)
                lhs[t * ROWS : (t + 1) * ROWS, a * DH : (a + 1) * DH] = moved * row_ok[a]
        conv = jnp.dot(lhs[...], band[h], preferred_element_type=jnp.float32)
        peak = jnp.full((ROWS, DH), -1e30, jnp.float32)
        lo, hi = row_lo[PAD:], row_hi[PAD:]
        for t in range(WINDOWS):
            place = lane + t * STEP
            kept = (place >= lo) & (place <= hi) & inner
            masked = jnp.where(kept, conv[t * ROWS : (t + 1) * ROWS], -1e30)
            conv_buf[t] = masked
            peak = jnp.maximum(peak, masked)
        peak = jnp.max(peak, axis=1, keepdims=True)
        total = jnp.zeros((ROWS, DH), jnp.float32)
        rows = pl.ds(pl.multiple_of(h * ROWS, ROWS), ROWS)
        for t in range(WINDOWS):
            weights = jnp.exp(conv_buf[t] - peak)
            total = total + weights
            probs[rows, t * DH : (t + 1) * DH] = weights.astype(jnp.bfloat16)
        total = jnp.sum(total, axis=1, keepdims=True)
        inv_total[h] = jnp.broadcast_to(1.0 / total, (ROWS, DH))

        @pl.when(h == 0)
        def _():
            after_four(2)
            after_four(3)

        @pl.when(h == 1)
        def _():
            after_one(2)
            after_one(3)

        @pl.when(h == 2)
        def _():
            after_five(2)
            after_five(3)

        return carry

    lax.fori_loop(0, GROUP, head, 0)
    last_two(2)
    last_two(3)
    for t in range(WINDOWS):
        vext[t * DH : (t + 1) * DH] = vwin[t * STEP : t * STEP + DH]

    def mix_values(p, carry):
        rows = pl.ds(pl.multiple_of(p * ROWS, ROWS), ROWS)
        acc[rows] = jnp.dot(probs[rows], vext[...], preferred_element_type=jnp.float32)
        return carry

    lax.fori_loop(0, GROUP, mix_values, 0)
    for h in range(GROUP):
        attn = jnp.zeros((ROWS, DH), jnp.float32)
        for p in range(GROUP):
            piece = acc[p * ROWS : (p + 1) * ROWS, h * DH : (h + 1) * DH] * inv_total[p]
            attn = attn + mix_ref[h, p] * piece
        mean_sq = jnp.mean(attn * attn, axis=1, keepdims=True)
        scaled = attn * lax.rsqrt(mean_sq + 1e-06) * gain_ref[:, h * DH : (h + 1) * DH]
        normed[:, h * DH : (h + 1) * DH] = scaled.astype(jnp.bfloat16)

    loads[3].wait()

    def partial(k, side):
        group = ((y + k) % ring_y) * CORES + side
        cols = pl.ds(pl.multiple_of(group * COLS, COLS), COLS)
        return jnp.dot(normed[...], w_vmem[:, cols], preferred_element_type=jnp.float32)

    def to_twin(k):
        return pltpu.make_async_remote_copy(
            src_ref=core_out.at[k],
            dst_ref=core_in.at[k],
            send_sem=core_send.at[k],
            recv_sem=core_recv.at[k],
            device_id=twin,
            device_id_type=MESH,
        )

    def to_chip(k):
        return pltpu.make_async_remote_copy(
            src_ref=chip_out.at[k - 1],
            dst_ref=chip_in.at[k - 1],
            send_sem=chip_send.at[k - 1],
            recv_sem=chip_recv.at[k - 1],
            device_id=chip(k),
            device_id_type=MESH,
        )

    order = [2, 1, 3, 0] if ring_y == 4 else list(range(ring_y - 1, -1, -1))
    for k in order:
        core_out[k] = partial(k, 1 - core).astype(jnp.bfloat16)
        to_twin(k).start()
    for k in order:
        mine = partial(k, core).astype(jnp.bfloat16).astype(jnp.float32)
        to_twin(k).wait_recv()
        both = mine + core_in[k].astype(jnp.float32)
        if k:
            chip_out[k - 1] = both.astype(jnp.bfloat16)
            to_chip(k).start()
        else:
            acc[0:ROWS] = both
    result = acc[0:ROWS]
    for k in sorted(order[:-1], key=lambda k: k == 2):
        to_chip(k).wait_recv()
        result = result + chip_in[k - 1].astype(jnp.float32)
    out_ref[...] = result.astype(jnp.bfloat16)

    tail.wait_send()
    for kind in range(5):
        for chunk in range(4):
            message(kind, chunk).wait_send()
    for k in order:
        to_twin(k).wait_send()
        if k:
            to_chip(k).wait_send()


def solution(mesh):
    pb_size, ha_size = mesh.shape["pb"], mesh.shape["ha"]
    ring_y = ha_size // CORES
    bf16, f32 = jnp.bfloat16, jnp.float32

    def per_device(queries, keys, values, theta, mix, gain, out_weight, turn_lengths):
        hbm = pl.BlockSpec(memory_space=pl.ANY)
        vmem = pl.BlockSpec(memory_space=pltpu.VMEM)
        smem = pl.BlockSpec(memory_space=pltpu.SMEM)
        far = max(ring_y - 1, 1)
        return pl.pallas_call(
            functools.partial(kernel, pb_size, ha_size),
            out_shape=jax.ShapeDtypeStruct((ROWS, COLS), bf16),
            in_specs=[smem, hbm, hbm, hbm, vmem, smem, vmem, hbm],
            out_specs=vmem,
            scratch_shapes=[
                pltpu.VMEM((QROWS, COLS), bf16),
                pltpu.VMEM((SPAN, COLS), bf16),
                pltpu.VMEM((SPAN, COLS), bf16),
                pltpu.VMEM(out_weight.shape, bf16),
                pltpu.VMEM((GROUP, 8, DH), f32),
                pltpu.VMEM((GROUP, QCONV * DH, DH), bf16),
                pltpu.VMEM((QROWS, DH), jnp.int32),
                pltpu.VMEM((QROWS, DH), jnp.int32),
                pltpu.VMEM((QCONV, ROWS, DH), bf16),
                pltpu.VMEM((WINDOWS, QROWS, DH), f32),
                pltpu.VMEM((WINDOWS * ROWS, QCONV * DH), bf16),
                pltpu.VMEM((WINDOWS, ROWS, DH), f32),
                pltpu.VMEM((GROUP * ROWS, WINDOWS * DH), bf16),
                pltpu.VMEM((GROUP, ROWS, DH), f32),
                pltpu.VMEM((WINDOWS * DH, COLS), bf16),
                pltpu.VMEM((GROUP * ROWS, COLS), f32),
                pltpu.VMEM((ROWS, COLS), bf16),
                pltpu.VMEM((ring_y, ROWS, COLS), bf16),
                pltpu.VMEM((ring_y, ROWS, COLS), bf16),
                pltpu.VMEM((far, ROWS, COLS), bf16),
                pltpu.VMEM((far, ROWS, COLS), bf16),
                pltpu.SemaphoreType.DMA((4,)),
                pltpu.SemaphoreType.DMA((2,)),
                pltpu.SemaphoreType.DMA((5, 4)),
                pltpu.SemaphoreType.DMA((5, 4)),
                pltpu.SemaphoreType.DMA((ring_y,)),
                pltpu.SemaphoreType.DMA((ring_y,)),
                pltpu.SemaphoreType.DMA((far,)),
                pltpu.SemaphoreType.DMA((far,)),
            ],
            compiler_params=pltpu.CompilerParams(
                collective_id=0, has_side_effects=True, vmem_limit_bytes=48 * 1024 * 1024
            ),
        )(turn_lengths, queries, keys, values, theta, mix, gain.reshape(1, COLS), out_weight)

    return jax.shard_map(
        per_device,
        mesh=mesh,
        in_specs=(
            P("pb", "ha"),
            P("pb", "ha"),
            P("pb", "ha"),
            P("ha", None, None),
            P("ha", None),
            P("ha"),
            P("ha", None),
            P(),
        ),
        out_specs=P("pb", "ha"),
        check_vma=False,
    )
```

profile of v0, /device:TPU:1, one launch (start us, length us, event | category | flops | bytes accessed | tf_op | source)
XLA Modules:
  0.0 52.7 jit_solution(14258782172075206291)
XLA Ops:
  0.0 0.7 %copy.9.theta_ref = f32[4,6,11]{2,1,0:T(8,128)S(1)} copy(f32[4,6,11]{2,0,1:T(4,128)} %param.11) | data formatting | bytes 2112 | tf_op args[3]
  0.7 0.0 copy-start
  0.7 2.2 %copy-done = bf16[512,4096]{1,0:T(8,128)(2,1)S(1)} copy-done((bf16[512,4096]{1,0:T(8,128)(2,1)S(1)}, bf16[512,4096]{1,0:T(8,128)(2,1)}, u32[]{:S(2)}) %copy-start) | copy-done | bytes 4194328
  2.9 0.0 copy-start.1
  2.9 0.9 %copy-done.1 = bf16[128,512]{1,0:T(8,128)(2,1)S(1)} copy-done((bf16[128,512]{1,0:T(8,128)(2,1)S(1)}, bf16[128,512]{1,0:T(8,128)(2,1)}, u32[]{:S(2)}) %copy-start.1) | copy-done | bytes 131096
  3.8 0.0 copy-start.2
  3.8 0.9 %copy-done.2 = bf16[128,512]{1,0:T(8,128)(2,1)S(1)} copy-done((bf16[128,512]{1,0:T(8,128)(2,1)S(1)}, bf16[128,512]{1,0:T(8,128)(2,1)}, u32[]{:S(2)}) %copy-start.2) | copy-done | bytes 131096
  4.7 0.0 copy-start.3
  4.7 0.9 %copy-done.3 = bf16[128,512]{1,0:T(8,128)(2,1)S(1)} copy-done((bf16[128,512]{1,0:T(8,128)(2,1)S(1)}, bf16[128,512]{1,0:T(8,128)(2,1)}, u32[]{:S(2)}) %copy-start.3) | copy-done | bytes 131096
  5.6 0.0 copy-start.4
  5.6 0.7 %copy-done.4 = f32[4,4]{1,0:T(4,128)S(1)} copy-done((f32[4,4]{1,0:T(4,128)S(1)}, f32[4,4]{1,0:T(4,128)}, u32[]{:S(2)}) %copy-start.4) | copy-done | bytes 88
  6.3 0.0 copy-start.5
  6.3 0.7 %copy-done.5 = f32[512]{0:T(512)S(1)} copy-done((f32[512]{0:T(512)S(1)}, f32[512]{0:T(512)}, u32[]{:S(2)}) %copy-start.5) | copy-done | bytes 2072
  7.0 0.0 copy-start.6
  7.0 0.7 %copy-done.6 = s32[16]{0:T(128)S(1)} copy-done((s32[16]{0:T(128)S(1)}, s32[16]{0:T(128)}, u32[]{:S(2)}) %copy-start.6) | copy-done | bytes 88
  7.6 44.4 %shard_map.82 = bf16[128,512]{1,0:T(8,128)(2,1)S(1)} custom-call(s32[16]{0:T(128)S(1)} %copy-done.6, bf16[128,512]{1,0:T(8,128)(2,1)S(1)} %copy-done.1, bf16[128,512]{1,0:T(8,128)(2,1)S(1)} %copy-done.2, bf16[128,512]{1,0:T(8,128)(2,1)S(1)} %copy-done.3, f32[4,6,11]{2,1,0:T(8,128)S(1)} %copy.9.theta_ref, f32[4,4]{1,0:T(4,128)S(1)} %copy-done.4, ...), custom_call_target="tpu_custom_call" | custom-call | tf_op jit(solution)/shard_map/pallas_call | solution.py:374
  52.1 0.7 %copy.11 = bf16[128,512]{1,0:T(8,128)(2,1)} copy(bf16[128,512]{1,0:T(8,128)(2,1)S(1)} %shard_map.82) | data formatting | bytes 262144
Async XLA Ops:
  0.7 2.2 %copy-start = (bf16[512,4096]{1,0:T(8,128)(2,1)S(1)}, bf16[512,4096]{1,0:T(8,128)(2,1)}, u32[]{:S(2)}) copy-start(bf16[512,4096]{1,0:T(8,128)(2,1)} %w_hbm.1) | copy-start | bytes 12582916
  2.9 0.9 %copy-start.1 = (bf16[128,512]{1,0:T(8,128)(2,1)S(1)}, bf16[128,512]{1,0:T(8,128)(2,1)}, u32[]{:S(2)}) copy-start(bf16[128,512]{1,0:T(8,128)(2,1)} %q_hbm.1) | copy-start | bytes 393220
  3.8 0.9 %copy-start.2 = (bf16[128,512]{1,0:T(8,128)(2,1)S(1)}, bf16[128,512]{1,0:T(8,128)(2,1)}, u32[]{:S(2)}) copy-start(bf16[128,512]{1,0:T(8,128)(2,1)} %k_hbm.1) | copy-start | bytes 393220
  4.7 0.9 %copy-start.3 = (bf16[128,512]{1,0:T(8,128)(2,1)S(1)}, bf16[128,512]{1,0:T(8,128)(2,1)}, u32[]{:S(2)}) copy-start(bf16[128,512]{1,0:T(8,128)(2,1)} %v_hbm.1) | copy-start | bytes 393220
  5.6 0.7 %copy-start.4 = (f32[4,4]{1,0:T(4,128)S(1)}, f32[4,4]{1,0:T(4,128)}, u32[]{:S(2)}) copy-start(f32[4,4]{1,0:T(4,128)} %mix_ref.1) | copy-start | bytes 196
  6.3 0.7 %copy-start.5 = (f32[512]{0:T(512)S(1)}, f32[512]{0:T(512)}, u32[]{:S(2)}) copy-start(f32[512]{0:T(512)} %param.13) | copy-start | bytes 6148
  7.0 0.7 %copy-start.6 = (s32[16]{0:T(128)S(1)}, s32[16]{0:T(128)}, u32[]{:S(2)}) copy-start(s32[16]{0:T(128)} %turns_ref.1) | copy-start | bytes 196
where the time goes:
time: 53 us; the launch traced here: 52.7 us
  Pallas kernels  44.4 us (84%)
  local copies, waits for them, and re-layouts  8.28 us (16%)
    pallas_call x1, Pallas kernels, per_device(): pl.pallas_call(functools.partial(kernel, pb_size, ha_size), out_shape=jax...  44.4 us
    unnamed x16, local copies, waits for them, and re-layouts  8.28 us

commit v1 on v0

v1 whole, which is shorter than its diff:
```python
import functools
import math

import jax
import jax.numpy as jnp
from jax import lax
from jax.experimental import pallas as pl
from jax.experimental.pallas import tpu as pltpu
from jax.sharding import PartitionSpec as P

GROUP = 4
QCONV = 6
KCONV = 11
REACH = (KCONV - 1) // 2
MAXBACK = 5
ROWS = 128
DH = 128
COLS = GROUP * DH
RING_X = 4
CORES = 2
PAD = 16
STEP = 112
WINDOWS = 7
SPAN = PAD + (MAXBACK + 1) * ROWS + PAD
QROWS = PAD + ROWS
HALF = ROWS // 2
MESH = pl.DeviceIdType.MESH
FOUR, ONE, TWO, THREE, FIVE = range(5)
FAR = 2


def slot_row(distance):
    return PAD + (MAXBACK - distance) * ROWS


def kernel(
    pb_size,
    ha_size,
    turns_hbm,
    q_hbm,
    k_hbm,
    v_hbm,
    theta_hbm,
    mix_hbm,
    gain_hbm,
    w_hbm,
    out_ref,
    turns_ref,
    theta_ref,
    mix_ref,
    gain_ref,
    qext,
    kwin,
    vwin,
    w_vmem,
    taps,
    band,
    row_lo,
    row_hi,
    row_ok,
    shifted,
    lhs,
    conv_buf,
    probs,
    inv_total,
    vext,
    acc,
    normed,
    core_out,
    core_in,
    chip_out,
    chip_in,
    q_behind,
    load_sem,
    tail_send,
    tail_recv,
    send_sem,
    recv_sem,
    core_send,
    core_recv,
    chip_send,
    chip_recv,
):
    pb = lax.axis_index("pb")
    ha = lax.axis_index("ha")
    ring_z = pb_size // RING_X
    ring_y = ha_size // CORES
    x, z = pb % RING_X, pb // RING_X
    core, y = ha % CORES, ha // CORES

    def at(new_z, new_x):
        return ((new_z % ring_z) * RING_X + new_x % RING_X, ha)

    x_next, x_over, x_back = at(z, x + 1), at(z, x + 2), at(z, x + RING_X - 1)
    z_next, z_back = at(z + 1, x), at(z + ring_z - 1, x)
    twin = (pb, y * CORES + 1 - core)

    def chip(k):
        return (pb, ((y + k) % ring_y) * CORES + core)

    own = slot_row(0)
    loads = [
        pltpu.make_async_copy(k_hbm, kwin.at[pl.ds(own, ROWS)], load_sem.at[0]),
        pltpu.make_async_copy(v_hbm, vwin.at[pl.ds(own, ROWS)], load_sem.at[1]),
        pltpu.make_async_copy(q_hbm, qext.at[pl.ds(PAD, ROWS)], load_sem.at[2]),
        pltpu.make_async_copy(turns_hbm, turns_ref, load_sem.at[4]),
        pltpu.make_async_copy(theta_hbm, theta_ref, load_sem.at[5]),
        pltpu.make_async_copy(mix_hbm, mix_ref, load_sem.at[6]),
        pltpu.make_async_copy(gain_hbm, gain_ref, load_sem.at[7]),
        pltpu.make_async_copy(w_hbm, w_vmem, load_sem.at[3]),
    ]
    for load in loads:
        load.start()

    barrier = pltpu.get_barrier_semaphore()
    greeted = [x_next, x_over, x_back, z_next, z_back, twin]
    greeted += [chip(k) for k in range(1, ring_y)]
    for other in greeted:
        pl.semaphore_signal(barrier, inc=1, device_id=other, device_id_type=MESH)
    pl.semaphore_wait(barrier, len(greeted))

    def message(kind, chunk):
        win = kwin if chunk < 2 else vwin
        shift = (chunk % 2) * HALF
        behind = slot_row(4)
        src, dst, target = {
            FOUR: (own, slot_row(4), z_next),
            ONE: (jnp.where(x < 3, own, behind), slot_row(1), x_next),
            TWO: (jnp.where(x < 2, own, behind), slot_row(2), x_over),
            THREE: (jnp.where(x < 1, own, behind), slot_row(3), x_back),
            FIVE: (slot_row(1), slot_row(5), z_next),
        }[kind]
        return pltpu.make_async_remote_copy(
            src_ref=win.at[pl.ds(pl.multiple_of(src + shift, 16), HALF)],
            dst_ref=win.at[pl.ds(dst + shift, HALF)],
            send_sem=send_sem.at[kind, chunk],
            recv_sem=recv_sem.at[kind, chunk],
            device_id=target,
            device_id_type=MESH,
        )

    def tail_copy(src, dst, n, target):
        return pltpu.make_async_remote_copy(
            src_ref=src,
            dst_ref=dst,
            send_sem=tail_send.at[n],
            recv_sem=tail_recv.at[n],
            device_id=target,
            device_id_type=MESH,
        )

    tail_z = tail_copy(qext.at[pl.ds(ROWS, PAD)], q_behind, 0, z_next)
    tail_own = tail_copy(qext.at[pl.ds(ROWS, PAD)], qext.at[pl.ds(0, PAD)], 1, x_next)
    tail_behind = tail_copy(q_behind, qext.at[pl.ds(0, PAD)], 1, x_next)

    def from_own(chunk):
        for kind, bound in ((ONE, 3), (TWO, 2), (THREE, 1)):

            @pl.when(x < bound)
            def _(kind=kind):
                message(kind, chunk).start()

    def from_behind(chunk):
        message(FOUR, chunk).wait_recv()
        for kind, bound in ((ONE, 3), (TWO, 2), (THREE, 1)):

            @pl.when(x >= bound)
            def _(kind=kind):
                message(kind, chunk).start()

    def to_five(chunk):
        message(ONE, chunk).wait_recv()
        message(FIVE, chunk).start()

    loads[0].wait()
    for chunk in (0, 1):
        message(FOUR, chunk).start()
        from_own(chunk)
    loads[2].wait()
    tail_z.start()

    @pl.when(x < 3)
    def _():
        tail_own.start()

    loads[1].wait()
    for chunk in (2, 3):
        message(FOUR, chunk).start()
    loads[3].wait()
    loads[4].wait()
    first_row = pb * ROWS
    for win in (kwin, vwin):
        win[0:PAD] = jnp.zeros((PAD, COLS), jnp.bfloat16)
        win[SPAN - PAD : SPAN] = jnp.zeros((PAD, COLS), jnp.bfloat16)
    pos = first_row - PAD + lax.broadcasted_iota(jnp.int32, (QROWS, DH), 0)
    row_start = jnp.zeros((QROWS, DH), jnp.int32)
    start = jnp.int32(0)
    for n in range(turns_ref.shape[0]):
        row_start = jnp.where(pos >= start, start, row_start)
        start = start + turns_ref[n]
    key_zero = first_row - slot_row(0)
    row_lo[...] = row_start - key_zero
    row_hi[...] = pos - key_zero
    rel = (pos - row_start)[PAD:]
    for a in range(QCONV):
        row_ok[a] = jnp.where(rel >= a, 1.0, 0.0).astype(jnp.bfloat16)
    taps[...] = jnp.zeros(taps.shape, jnp.float32)
    scaled_theta = theta_ref[...] * (1.0 / math.sqrt(DH))
    taps[:, 0:GROUP, 0 : REACH + 1] = scaled_theta[:, :, REACH:]
    taps[:, 0:GROUP, DH - REACH : DH] = scaled_theta[:, :, :REACH]

    for chunk in (0, 1):
        from_behind(chunk)
    tail_z.wait_recv()

    @pl.when(x == 3)
    def _():
        tail_behind.start()

    for chunk in (2, 3):
        from_own(chunk)

    def make_band(h, carry):
        for a in range(QCONV):
            line = jnp.broadcast_to(taps[a, pl.ds(h, 1), :], (DH, DH))
            square = pltpu.roll(line, 0, 1, stride=1, stride_axis=0)
            band[h, a * DH : (a + 1) * DH, :] = square.astype(jnp.bfloat16)
        return carry

    lax.fori_loop(0, GROUP, make_band, 0)
    to_five(0)
    to_five(1)
    from_behind(2)
    from_behind(3)
    tail_own.wait_recv()
    for chunk in (0, 1):
        message(TWO, chunk).wait_recv()
        message(THREE, chunk).wait_recv()

    lane = lax.broadcasted_iota(jnp.int32, (ROWS, DH), 1)
    q_lane = lax.broadcasted_iota(jnp.int32, (QROWS, DH), 1)
    inner = (lane >= 8) & (lane < 8 + STEP)

    def convolve(h, windows):
        cols = pl.ds(pl.multiple_of(h * DH, DH), DH)
        q_head = qext[:, cols]
        for t in windows:
            k_head = kwin[t * STEP : t * STEP + DH, cols]
            scores = lax.dot_general(
                q_head, k_head, (((1,), (1,)), ((), ())), preferred_element_type=jnp.float32
            )
            place = q_lane + t * STEP
            seen = (place >= row_lo[...]) & (place <= row_hi[...])
            shifted[t] = jnp.where(seen, scores, 0.0)
        for t in windows:
            for a in range(QCONV):
                moved = shifted[t, PAD - a : PAD - a + ROWS, :].astype(jnp.bfloat16)
                lhs[t * ROWS : (t + 1) * ROWS, a * DH : (a + 1) * DH] = moved * row_ok[a]
        top, end = windows[0], windows[-1] + 1
        conv = jnp.dot(
            lhs[top * ROWS : end * ROWS], band[h], preferred_element_type=jnp.float32
        )
        lo, hi = row_lo[PAD:], row_hi[PAD:]
        for t in windows:
            place = lane + t * STEP
            kept = (place >= lo) & (place <= hi) & inner
            piece = conv[(t - top) * ROWS : (t - top + 1) * ROWS]
            conv_buf[h, t] = jnp.where(kept, piece, -1e30)

    near, far = list(range(FAR, WINDOWS)), list(range(FAR))

    def near_head(h, carry):
        convolve(h, near)
        for when, chunk in ((1, 2), (2, 3)):

            @pl.when((h == when) & (x > 0))
            def _(chunk=chunk):
                to_five(chunk)

        return carry

    lax.fori_loop(0, GROUP, near_head, 0)

    @pl.when(x == 0)
    def _():
        to_five(2)
        to_five(3)

    for chunk in (0, 1):
        message(FIVE, chunk).wait_recv()

    def far_head(h, carry):
        convolve(h, far)
        peak = conv_buf[h, 0]
        for t in range(1, WINDOWS):
            peak = jnp.maximum(peak, conv_buf[h, t])
        peak = jnp.max(peak, axis=1, keepdims=True)
        total = jnp.zeros((ROWS, DH), jnp.float32)
        rows = pl.ds(pl.multiple_of(h * ROWS, ROWS), ROWS)
        for t in range(WINDOWS):
            weights = jnp.exp(conv_buf[h, t] - peak)
            total = total + weights
            probs[rows, t * DH : (t + 1) * DH] = weights.astype(jnp.bfloat16)
        total = jnp.sum(total, axis=1, keepdims=True)
        inv_total[h] = jnp.broadcast_to(1.0 / total, (ROWS, DH))
        return carry

    lax.fori_loop(0, GROUP, far_head, 0)
    split = FAR * DH
    for chunk in (2, 3):
        message(TWO, chunk).wait_recv()
        message(THREE, chunk).wait_recv()
    for t in near:
        vext[t * DH : (t + 1) * DH] = vwin[t * STEP : t * STEP + DH]

    def near_values(p, carry):
        rows = pl.ds(pl.multiple_of(p * ROWS, ROWS), ROWS)
        acc[rows] = jnp.dot(
            probs[rows, split:], vext[split:], preferred_element_type=jnp.float32
        )
        return carry

    lax.fori_loop(0, GROUP, near_values, 0)
    for chunk in (2, 3):
        message(FIVE, chunk).wait_recv()
    for t in far:
        vext[t * DH : (t + 1) * DH] = vwin[t * STEP : t * STEP + DH]

    def far_values(p, carry):
        rows = pl.ds(pl.multiple_of(p * ROWS, ROWS), ROWS)
        acc[rows] += jnp.dot(
            probs[rows, :split], vext[:split], preferred_element_type=jnp.float32
        )
        return carry

    lax.fori_loop(0, GROUP, far_values, 0)
    for load in loads[5:]:
        load.wait()
    for h in range(GROUP):
        attn = jnp.zeros((ROWS, DH), jnp.float32)
        for p in range(GROUP):
            piece = acc[p * ROWS : (p + 1) * ROWS, h * DH : (h + 1) * DH] * inv_total[p]
            attn = attn + mix_ref[h, p] * piece
        mean_sq = jnp.mean(attn * attn, axis=1, keepdims=True)
        scaled = attn * lax.rsqrt(mean_sq + 1e-06) * gain_ref[:, h * DH : (h + 1) * DH]
        normed[:, h * DH : (h + 1) * DH] = scaled.astype(jnp.bfloat16)

    def partial(k, side):
        group = ((y + k) % ring_y) * CORES + side
        cols = pl.ds(pl.multiple_of(group * COLS, COLS), COLS)
        return jnp.dot(normed[...], w_vmem[:, cols], preferred_element_type=jnp.float32)

    def to_twin(k):
        return pltpu.make_async_remote_copy(
            src_ref=core_out.at[k],
            dst_ref=core_in.at[k],
            send_sem=core_send.at[k],
            recv_sem=core_recv.at[k],
            device_id=twin,
            device_id_type=MESH,
        )

    def to_chip(k):
        return pltpu.make_async_remote_copy(
            src_ref=chip_out.at[k - 1],
            dst_ref=chip_in.at[k - 1],
            send_sem=chip_send.at[k - 1],
            recv_sem=chip_recv.at[k - 1],
            device_id=chip(k),
            device_id_type=MESH,
        )

    order = [2, 1, 3, 0] if ring_y == 4 else list(range(ring_y - 1, -1, -1))
    for k in order:
        core_out[k] = partial(k, 1 - core).astype(jnp.bfloat16)
        to_twin(k).start()
    for k in order:
        mine = partial(k, core).astype(jnp.bfloat16).astype(jnp.float32)
        to_twin(k).wait_recv()
        both = mine + core_in[k].astype(jnp.float32)
        if k:
            chip_out[k - 1] = both.astype(jnp.bfloat16)
            to_chip(k).start()
        else:
            acc[0:ROWS] = both
    result = acc[0:ROWS]
    for k in sorted(order[:-1], key=lambda k: k == 2):
        to_chip(k).wait_recv()
        result = result + chip_in[k - 1].astype(jnp.float32)
    out_ref[...] = result.astype(jnp.bfloat16)

    tail_z.wait_send()
    tail_own.wait_send()
    for kind in range(5):
        for chunk in range(4):
            message(kind, chunk).wait_send()
    for k in order:
        to_twin(k).wait_send()
        if k:
            to_chip(k).wait_send()


def solution(mesh):
    pb_size, ha_size = mesh.shape["pb"], mesh.shape["ha"]
    ring_y = ha_size // CORES
    bf16, f32 = jnp.bfloat16, jnp.float32

    def per_device(queries, keys, values, theta, mix, gain, out_weight, turn_lengths):
        hbm = pl.BlockSpec(memory_space=pltpu.HBM)
        vmem = pl.BlockSpec(memory_space=pltpu.VMEM)
        far = max(ring_y - 1, 1)
        return pl.pallas_call(
            functools.partial(kernel, pb_size, ha_size),
            out_shape=jax.ShapeDtypeStruct((ROWS, COLS), bf16),
            in_specs=[hbm] * 8,
            out_specs=vmem,
            scratch_shapes=[
                pltpu.SMEM(turn_lengths.shape, jnp.int32),
                pltpu.VMEM((QCONV, GROUP, KCONV), f32),
                pltpu.SMEM(mix.shape, f32),
                pltpu.VMEM((1, COLS), f32),
                pltpu.VMEM((QROWS, COLS), bf16),
                pltpu.VMEM((SPAN, COLS), bf16),
                pltpu.VMEM((SPAN, COLS), bf16),
                pltpu.VMEM(out_weight.shape, bf16),
                pltpu.VMEM((QCONV, 8, DH), f32),
                pltpu.VMEM((GROUP, QCONV * DH, DH), bf16),
                pltpu.VMEM((QROWS, DH), jnp.int32),
                pltpu.VMEM((QROWS, DH), jnp.int32),
                pltpu.VMEM((QCONV, ROWS, DH), bf16),
                pltpu.VMEM((WINDOWS, QROWS, DH), f32),
                pltpu.VMEM((WINDOWS * ROWS, QCONV * DH), bf16),
                pltpu.VMEM((GROUP, WINDOWS, ROWS, DH), f32),
                pltpu.VMEM((GROUP * ROWS, WINDOWS * DH), bf16),
                pltpu.VMEM((GROUP, ROWS, DH), f32),
                pltpu.VMEM((WINDOWS * DH, COLS), bf16),
                pltpu.VMEM((GROUP * ROWS, COLS), f32),
                pltpu.VMEM((ROWS, COLS), bf16),
                pltpu.VMEM((ring_y, ROWS, COLS), bf16),
                pltpu.VMEM((ring_y, ROWS, COLS), bf16),
                pltpu.VMEM((far, ROWS, COLS), bf16),
                pltpu.VMEM((far, ROWS, COLS), bf16),
                pltpu.VMEM((PAD, COLS), bf16),
                pltpu.SemaphoreType.DMA((8,)),
                pltpu.SemaphoreType.DMA((2,)),
                pltpu.SemaphoreType.DMA((2,)),
                pltpu.SemaphoreType.DMA((5, 4)),
                pltpu.SemaphoreType.DMA((5, 4)),
                pltpu.SemaphoreType.DMA((ring_y,)),
                pltpu.SemaphoreType.DMA((ring_y,)),
                pltpu.SemaphoreType.DMA((far,)),
                pltpu.SemaphoreType.DMA((far,)),
            ],
            compiler_params=pltpu.CompilerParams(
                collective_id=0, has_side_effects=True, vmem_limit_bytes=56 * 1024 * 1024
            ),
        )(
            turn_lengths,
            queries,
            keys,
            values,
            jnp.transpose(theta, (1, 0, 2)),
            mix,
            gain.reshape(1, COLS),
            out_weight,
        )

    return jax.shard_map(
        per_device,
        mesh=mesh,
        in_specs=(
            P("pb", "ha"),
            P("pb", "ha"),
            P("pb", "ha"),
            P("ha", None, None),
            P("ha", None),
            P("ha"),
            P("ha", None),
            P(),
        ),
        out_specs=P("pb", "ha"),
        check_vma=False,
    )
```

time: 53 us -> 45.6 us (0.86)
  local copies, waits for them, and re-layouts: 8.28 us -> 1.57 us
    unnamed x16 -> x1, local copies, waits for them, and re-layouts: 8.28 us -> 1.57 us
where the time goes in v1:
time: 45.6 us; the launch traced here: 45.5 us
  Pallas kernels  43.9 us (96%)
  local copies, waits for them, and re-layouts  1.57 us (3%)
    pallas_call x1, Pallas kernels, per_device(): pl.pallas_call(functools.partial(kernel, pb_size, ha_size), out_shape=jax...  43.9 us
    unnamed x1, local copies, waits for them, and re-layouts  1.57 us

profile of v1, /device:TPU:1, one launch (start us, length us, event | category | flops | bytes accessed | tf_op | source)
XLA Modules:
  0.0 45.5 jit_solution(7788731372918029673)
XLA Ops:
  0.0 43.9 %shard_map.82 = bf16[128,512]{1,0:T(8,128)(2,1)} custom-call(s32[16]{0:T(128)} %turns_hbm.1, bf16[128,512]{1,0:T(8,128)(2,1)} %q_hbm.1, bf16[128,512]{1,0:T(8,128)(2,1)} %k_hbm.1, bf16[128,512]{1,0:T(8,128)(2,1)} %v_hbm.1, f32[6,4,11]{2,1,0:T(4,128)} %bitcast.2, f32[4,4]{1,0:T(4,128)} %mix_hbm.1, f32[1,512]{1,0:T(1,128)} %bitcast.3, bf16[512,4096]{1,0:T(8,128)(2,1)} %w_hbm.1), custom_call_target="tpu_custom_call" | custom-call | tf_op jit(solution)/shard_map/pallas_call | solution.py:412
  43.9 1.6 %copy.10 = bf16[128,512]{1,0:T(8,128)(2,1)} copy(bf16[128,512]{1,0:T(8,128)(2,1)} %shard_map.82) | data formatting | bytes 262144

commit v2 on v1

--- a/solution.py
+++ b/solution.py
@@ -113,11 +113,45 @@
         load.start()
 
     barrier = pltpu.get_barrier_semaphore()
-    greeted = [x_next, x_over, x_back, z_next, z_back, twin]
+    has_next, has_back = z < ring_z - 1, z > 0
+    greeted = [x_next, x_over, x_back, twin]
     greeted += [chip(k) for k in range(1, ring_y)]
+
+    def greet(other):
+        pl.semaphore_signal(barrier, inc=1, device_id=other, device_id_type=MESH)
+
     for other in greeted:
-        pl.semaphore_signal(barrier, inc=1, device_id=other, device_id_type=MESH)
-    pl.semaphore_wait(barrier, len(greeted))
+        greet(other)
+
+    @pl.when(has_next)
+    def _():
+        greet(z_next)
+
+    @pl.when(has_back)
+    def _():
+        greet(z_back)
+
+    for win in (kwin, vwin):
+        for distance in range(1, MAXBACK + 1):
+
+            @pl.when(pb < distance)
+            def _(win=win, row=slot_row(distance)):
+                win[row : row + ROWS] = jnp.zeros((ROWS, COLS), jnp.bfloat16)
+
+    @pl.when(pb < 1)
+    def _():
+        qext[0:PAD] = jnp.zeros((PAD, COLS), jnp.bfloat16)
+
+    pl.semaphore_wait(
+        barrier, len(greeted) + has_next.astype(jnp.int32) + has_back.astype(jnp.int32)
+    )
+
+    def arrived(kind, chunk):
+        distance = {ONE: 1, TWO: 2, THREE: 3, FOUR: 4, FIVE: 5}[kind]
+
+        @pl.when(pb >= distance)
+        def _():
+            message(kind, chunk).wait_recv()
 
     def message(kind, chunk):
         win = kwin if chunk < 2 else vwin
@@ -161,23 +195,34 @@
                 message(kind, chunk).start()
 
     def from_behind(chunk):
-        message(FOUR, chunk).wait_recv()
+        arrived(FOUR, chunk)
         for kind, bound in ((ONE, 3), (TWO, 2), (THREE, 1)):
 
-            @pl.when(x >= bound)
+            @pl.when((x >= bound) & has_back)
             def _(kind=kind):
                 message(kind, chunk).start()
 
+    def to_four(chunk):
+        @pl.when(has_next)
+        def _():
+            message(FOUR, chunk).start()
+
     def to_five(chunk):
-        message(ONE, chunk).wait_recv()
-        message(FIVE, chunk).start()
+        arrived(ONE, chunk)
+
+        @pl.when(has_next & (pb > 0))
+        def _():
+            message(FIVE, chunk).start()
 
     loads[0].wait()
     for chunk in (0, 1):
-        message(FOUR, chunk).start()
+        to_four(chunk)
         from_own(chunk)
     loads[2].wait()
-    tail_z.start()
+
+    @pl.when(has_next)
+    def _():
+        tail_z.start()
 
     @pl.when(x < 3)
     def _():
@@ -185,7 +230,7 @@
 
     loads[1].wait()
     for chunk in (2, 3):
-        message(FOUR, chunk).start()
+        to_four(chunk)
     loads[3].wait()
     loads[4].wait()
     first_row = pb * ROWS
@@ -211,9 +256,12 @@
 
     for chunk in (0, 1):
         from_behind(chunk)
-    tail_z.wait_recv()
-
-    @pl.when(x == 3)
+
+    @pl.when(has_back)
+    def _():
+        tail_z.wait_recv()
+
+    @pl.when((x == 3) & has_back)
     def _():
         tail_behind.start()
 
@@ -232,10 +280,14 @@
     to_five(1)
     from_behind(2)
     from_behind(3)
-    tail_own.wait_recv()
+
+    @pl.when(pb >= 1)
+    def _():
+        tail_own.wait_recv()
+
     for chunk in (0, 1):
-        message(TWO, chunk).wait_recv()
-        message(THREE, chunk).wait_recv()
+        arrived(TWO, chunk)
+        arrived(THREE, chunk)
 
     lane = lax.broadcasted_iota(jnp.int32, (ROWS, DH), 1)
     q_lane = lax.broadcasted_iota(jnp.int32, (QROWS, DH), 1)
@@ -287,7 +339,7 @@
         to_five(3)
 
     for chunk in (0, 1):
-        message(FIVE, chunk).wait_recv()
+        arrived(FIVE, chunk)
 
     def far_head(h, carry):
         convolve(h, far)
@@ -308,8 +360,8 @@
     lax.fori_loop(0, GROUP, far_head, 0)
     split = FAR * DH
     for chunk in (2, 3):
-        message(TWO, chunk).wait_recv()
-        message(THREE, chunk).wait_recv()
+        arrived(TWO, chunk)
+        arrived(THREE, chunk)
     for t in near:
         vext[t * DH : (t + 1) * DH] = vwin[t * STEP : t * STEP + DH]
 
@@ -322,7 +374,7 @@
 
     lax.fori_loop(0, GROUP, near_values, 0)
     for chunk in (2, 3):
-        message(FIVE, chunk).wait_recv()
+        arrived(FIVE, chunk)
     for t in far:
         vext[t * DH : (t + 1) * DH] = vwin[t * STEP : t * STEP + DH]
 
@@ -389,11 +441,28 @@
         result = result + chip_in[k - 1].astype(jnp.float32)
     out_ref[...] = result.astype(jnp.bfloat16)
 
-    tail_z.wait_send()
-    tail_own.wait_send()
-    for kind in range(5):
-        for chunk in range(4):
-            message(kind, chunk).wait_send()
+    sends = {
+        ONE: (x < 3) | has_back,
+        TWO: (x < 2) | has_back,
+        THREE: (x < 1) | has_back,
+        FOUR: has_next,
+        FIVE: has_next & (pb > 0),
+    }
+    for kind, sent in sends.items():
+
+        @pl.when(sent)
+        def _(kind=kind):
+            for chunk in range(4):
+                message(kind, chunk).wait_send()
+
+    @pl.when(has_next)
+    def _():
+        tail_z.wait_send()
+
+    @pl.when((x < 3) | has_back)
+    def _():
+        tail_own.wait_send()
+
     for k in order:
         to_twin(k).wait_send()
         if k:

time: 45.6 us -> 40.7 us (0.89)
  the two profiles are of different devices: /device:TPU:1 before, /device:TPU:161 now
where the time goes in v2:
time: 40.7 us; the launch traced here: 40.6 us
  Pallas kernels  39.1 us (96%)
  local copies, waits for them, and re-layouts  1.57 us (4%)
    pallas_call x1, Pallas kernels, per_device(): pl.pallas_call(functools.partial(kernel, pb_size, ha_size), out_shape=jax...  39.1 us
    unnamed x1, local copies, waits for them, and re-layouts  1.57 us

profile of v2, /device:TPU:161, one launch (start us, length us, event | category | flops | bytes accessed | tf_op | source)
XLA Modules:
  0.0 40.6 jit_solution(1083138286568739157)
XLA Ops:
  0.0 39.1 %shard_map.82 = bf16[128,512]{1,0:T(8,128)(2,1)} custom-call(s32[16]{0:T(128)} %turns_hbm.1, bf16[128,512]{1,0:T(8,128)(2,1)} %q_hbm.1, bf16[128,512]{1,0:T(8,128)(2,1)} %k_hbm.1, bf16[128,512]{1,0:T(8,128)(2,1)} %v_hbm.1, f32[6,4,11]{2,1,0:T(4,128)} %bitcast.2, f32[4,4]{1,0:T(4,128)} %mix_hbm.1, f32[1,512]{1,0:T(1,128)} %bitcast.3, bf16[512,4096]{1,0:T(8,128)(2,1)} %w_hbm.1), custom_call_target="tpu_custom_call" | custom-call | tf_op jit(solution)/shard_map/pallas_call | solution.py:481
  39.1 1.6 %copy.10 = bf16[128,512]{1,0:T(8,128)(2,1)} copy(bf16[128,512]{1,0:T(8,128)(2,1)} %shard_map.82) | data formatting | bytes 262144

commit v3 on v2

--- a/solution.py
+++ b/solution.py
@@ -23,10 +23,14 @@
 WINDOWS = 7
 SPAN = PAD + (MAXBACK + 1) * ROWS + PAD
 QROWS = PAD + ROWS
-HALF = ROWS // 2
 MESH = pl.DeviceIdType.MESH
-FOUR, ONE, TWO, THREE, FIVE = range(5)
+FOUR, ONE, TWO, THREE, FIVE, TWO_BACK = range(6)
+PHASES = ((6, 5, 2), (4, 3), (0, 1))
 FAR = 2
+CHUNKS = 4
+CHUNK = ROWS // CHUNKS
+KEY_CHUNKS = tuple(range(CHUNKS))
+VALUE_CHUNKS = tuple(range(CHUNKS, 2 * CHUNKS))
 
 
 def slot_row(distance):
@@ -154,8 +158,8 @@
             message(kind, chunk).wait_recv()
 
     def message(kind, chunk):
-        win = kwin if chunk < 2 else vwin
-        shift = (chunk % 2) * HALF
+        win = kwin if chunk < CHUNKS else vwin
+        shift = (chunk % CHUNKS) * CHUNK
         behind = slot_row(4)
         src, dst, target = {
             FOUR: (own, slot_row(4), z_next),
@@ -163,12 +167,15 @@
             TWO: (jnp.where(x < 2, own, behind), slot_row(2), x_over),
             THREE: (jnp.where(x < 1, own, behind), slot_row(3), x_back),
             FIVE: (slot_row(1), slot_row(5), z_next),
+            TWO_BACK: (slot_row(3), slot_row(2), x_back),
         }[kind]
+        if kind == TWO and chunk >= CHUNKS:
+            src, dst, target = slot_row(1), slot_row(2), x_next
         return pltpu.make_async_remote_copy(
-            src_ref=win.at[pl.ds(pl.multiple_of(src + shift, 16), HALF)],
-            dst_ref=win.at[pl.ds(dst + shift, HALF)],
+            src_ref=win.at[pl.ds(pl.multiple_of(src + shift, 16), CHUNK)],
+            dst_ref=win.at[pl.ds(dst + shift, CHUNK)],
             send_sem=send_sem.at[kind, chunk],
-            recv_sem=recv_sem.at[kind, chunk],
+            recv_sem=recv_sem.at[TWO if kind == TWO_BACK else kind, chunk],
             device_id=target,
             device_id_type=MESH,
         )
@@ -187,8 +194,12 @@
     tail_own = tail_copy(qext.at[pl.ds(ROWS, PAD)], qext.at[pl.ds(0, PAD)], 1, x_next)
     tail_behind = tail_copy(q_behind, qext.at[pl.ds(0, PAD)], 1, x_next)
 
+    def steps(chunk):
+        two = ((TWO, 2),) if chunk < CHUNKS else ()
+        return ((ONE, 3), *two, (THREE, 1))
+
     def from_own(chunk):
-        for kind, bound in ((ONE, 3), (TWO, 2), (THREE, 1)):
+        for kind, bound in steps(chunk):
 
             @pl.when(x < bound)
             def _(kind=kind):
@@ -196,7 +207,7 @@
 
     def from_behind(chunk):
         arrived(FOUR, chunk)
-        for kind, bound in ((ONE, 3), (TWO, 2), (THREE, 1)):
+        for kind, bound in steps(chunk):
 
             @pl.when((x >= bound) & has_back)
             def _(kind=kind):
@@ -214,8 +225,19 @@
         def _():
             message(FIVE, chunk).start()
 
+    def to_two(chunk):
+        @pl.when((x < 3) & (pb > 0))
+        def _():
+            message(TWO, chunk).start()
+
+    def back_to_two(chunk):
+        @pl.when((x == 1) & has_back)
+        def _():
+            message(THREE, chunk).wait_recv()
+            message(TWO_BACK, chunk).start()
+
     loads[0].wait()
-    for chunk in (0, 1):
+    for chunk in KEY_CHUNKS:
         to_four(chunk)
         from_own(chunk)
     loads[2].wait()
@@ -229,7 +251,7 @@
         tail_own.start()
 
     loads[1].wait()
-    for chunk in (2, 3):
+    for chunk in VALUE_CHUNKS:
         to_four(chunk)
     loads[3].wait()
     loads[4].wait()
@@ -254,7 +276,7 @@
     taps[:, 0:GROUP, 0 : REACH + 1] = scaled_theta[:, :, REACH:]
     taps[:, 0:GROUP, DH - REACH : DH] = scaled_theta[:, :, :REACH]
 
-    for chunk in (0, 1):
+    for chunk in KEY_CHUNKS:
         from_behind(chunk)
 
     @pl.when(has_back)
@@ -265,7 +287,7 @@
     def _():
         tail_behind.start()
 
-    for chunk in (2, 3):
+    for chunk in VALUE_CHUNKS:
         from_own(chunk)
 
     def make_band(h, carry):
@@ -276,116 +298,100 @@
         return carry
 
     lax.fori_loop(0, GROUP, make_band, 0)
-    to_five(0)
-    to_five(1)
-    from_behind(2)
-    from_behind(3)
+    for chunk in KEY_CHUNKS:
+        to_five(chunk)
 
     @pl.when(pb >= 1)
     def _():
         tail_own.wait_recv()
-
-    for chunk in (0, 1):
-        arrived(TWO, chunk)
-        arrived(THREE, chunk)
 
     lane = lax.broadcasted_iota(jnp.int32, (ROWS, DH), 1)
     q_lane = lax.broadcasted_iota(jnp.int32, (QROWS, DH), 1)
     inner = (lane >= 8) & (lane < 8 + STEP)
 
-    def convolve(h, windows):
-        cols = pl.ds(pl.multiple_of(h * DH, DH), DH)
-        q_head = qext[:, cols]
-        for t in windows:
-            k_head = kwin[t * STEP : t * STEP + DH, cols]
-            scores = lax.dot_general(
-                q_head, k_head, (((1,), (1,)), ((), ())), preferred_element_type=jnp.float32
+    def convolve(windows):
+        for h in range(GROUP):
+            q_head = qext[:, h * DH : (h + 1) * DH]
+            for t in windows:
+                k_head = kwin[t * STEP : t * STEP + DH, h * DH : (h + 1) * DH]
+                scores = lax.dot_general(
+                    q_head,
+                    k_head,
+                    (((1,), (1,)), ((), ())),
+                    preferred_element_type=jnp.float32,
+                )
+                place = q_lane + t * STEP
+                seen = (place >= row_lo[...]) & (place <= row_hi[...])
+                shifted[h, t] = jnp.where(seen, scores, 0.0)
+        for h in range(GROUP):
+            for n, t in enumerate(windows):
+                for a in range(QCONV):
+                    moved = shifted[h, t, PAD - a : PAD - a + ROWS, :].astype(jnp.bfloat16)
+                    lhs[h, n * ROWS : (n + 1) * ROWS, a * DH : (a + 1) * DH] = (
+                        moved * row_ok[a]
+                    )
+        lo, hi = row_lo[PAD:], row_hi[PAD:]
+        for h in range(GROUP):
+            conv = jnp.dot(
+                lhs[h, : len(windows) * ROWS], band[h], preferred_element_type=jnp.float32
             )
-            place = q_lane + t * STEP
-            seen = (place >= row_lo[...]) & (place <= row_hi[...])
-            shifted[t] = jnp.where(seen, scores, 0.0)
-        for t in windows:
-            for a in range(QCONV):
-                moved = shifted[t, PAD - a : PAD - a + ROWS, :].astype(jnp.bfloat16)
-                lhs[t * ROWS : (t + 1) * ROWS, a * DH : (a + 1) * DH] = moved * row_ok[a]
-        top, end = windows[0], windows[-1] + 1
-        conv = jnp.dot(
-            lhs[top * ROWS : end * ROWS], band[h], preferred_element_type=jnp.float32
-        )
-        lo, hi = row_lo[PAD:], row_hi[PAD:]
-        for t in windows:
-            place = lane + t * STEP
-            kept = (place >= lo) & (place <= hi) & inner
-            piece = conv[(t - top) * ROWS : (t - top + 1) * ROWS]
-            conv_buf[h, t] = jnp.where(kept, piece, -1e30)
-
-    near, far = list(range(FAR, WINDOWS)), list(range(FAR))
-
-    def near_head(h, carry):
-        convolve(h, near)
-        for when, chunk in ((1, 2), (2, 3)):
-
-            @pl.when((h == when) & (x > 0))
-            def _(chunk=chunk):
-                to_five(chunk)
-
-        return carry
-
-    lax.fori_loop(0, GROUP, near_head, 0)
-
-    @pl.when(x == 0)
-    def _():
-        to_five(2)
-        to_five(3)
-
-    for chunk in (0, 1):
+            for n, t in enumerate(windows):
+                place = lane + t * STEP
+                kept = (place >= lo) & (place <= hi) & inner
+                piece = conv[n * ROWS : (n + 1) * ROWS]
+                conv_buf[h, t] = jnp.where(kept, piece, -1e30)
+
+    near, far = range(FAR, WINDOWS), range(FAR)
+
+    for chunk in VALUE_CHUNKS:
+        from_behind(chunk)
+    for chunk in KEY_CHUNKS:
+        arrived(THREE, chunk)
+    convolve(PHASES[0])
+    for chunk in VALUE_CHUNKS:
+        to_five(chunk)
+        to_two(chunk)
+    for chunk in VALUE_CHUNKS:
+        back_to_two(chunk)
+    for chunk in KEY_CHUNKS:
+        arrived(TWO, chunk)
+    convolve(PHASES[1])
+    for chunk in KEY_CHUNKS:
         arrived(FIVE, chunk)
 
-    def far_head(h, carry):
-        convolve(h, far)
+    convolve(PHASES[2])
+    for h in range(GROUP):
         peak = conv_buf[h, 0]
         for t in range(1, WINDOWS):
             peak = jnp.maximum(peak, conv_buf[h, t])
         peak = jnp.max(peak, axis=1, keepdims=True)
         total = jnp.zeros((ROWS, DH), jnp.float32)
-        rows = pl.ds(pl.multiple_of(h * ROWS, ROWS), ROWS)
         for t in range(WINDOWS):
             weights = jnp.exp(conv_buf[h, t] - peak)
             total = total + weights
-            probs[rows, t * DH : (t + 1) * DH] = weights.astype(jnp.bfloat16)
+            probs[h * ROWS : (h + 1) * ROWS, t * DH : (t + 1) * DH] = weights.astype(
+                jnp.bfloat16
+            )
         total = jnp.sum(total, axis=1, keepdims=True)
         inv_total[h] = jnp.broadcast_to(1.0 / total, (ROWS, DH))
-        return carry
-
-    lax.fori_loop(0, GROUP, far_head, 0)
     split = FAR * DH
-    for chunk in (2, 3):
+    for chunk in VALUE_CHUNKS:
         arrived(TWO, chunk)
-        arrived(THREE, chunk)
+
+        @pl.when((pb >= 3) & (x != 1))
+        def _(chunk=chunk):
+            message(THREE, chunk).wait_recv()
+
     for t in near:
         vext[t * DH : (t + 1) * DH] = vwin[t * STEP : t * STEP + DH]
 
-    def near_values(p, carry):
-        rows = pl.ds(pl.multiple_of(p * ROWS, ROWS), ROWS)
-        acc[rows] = jnp.dot(
-            probs[rows, split:], vext[split:], preferred_element_type=jnp.float32
-        )
-        return carry
-
-    lax.fori_loop(0, GROUP, near_values, 0)
-    for chunk in (2, 3):
+    acc[...] = jnp.dot(probs[:, split:], vext[split:], preferred_element_type=jnp.float32)
+    for chunk in VALUE_CHUNKS:
         arrived(FIVE, chunk)
     for t in far:
         vext[t * DH : (t + 1) * DH] = vwin[t * STEP : t * STEP + DH]
 
-    def far_values(p, carry):
-        rows = pl.ds(pl.multiple_of(p * ROWS, ROWS), ROWS)
-        acc[rows] += jnp.dot(
-            probs[rows, :split], vext[:split], preferred_element_type=jnp.float32
-        )
-        return carry
-
-    lax.fori_loop(0, GROUP, far_values, 0)
+    acc[...] += jnp.dot(probs[:, :split], vext[:split], preferred_element_type=jnp.float32)
     for load in loads[5:]:
         load.wait()
     for h in range(GROUP):
@@ -429,30 +435,33 @@
     for k in order:
         mine = partial(k, core).astype(jnp.bfloat16).astype(jnp.float32)
         to_twin(k).wait_recv()
-        both = mine + core_in[k].astype(jnp.float32)
+        pair = mine + core_in[k].astype(jnp.float32)
         if k:
-            chip_out[k - 1] = both.astype(jnp.bfloat16)
+            chip_out[k - 1] = pair.astype(jnp.bfloat16)
             to_chip(k).start()
         else:
-            acc[0:ROWS] = both
+            acc[0:ROWS] = pair
     result = acc[0:ROWS]
     for k in sorted(order[:-1], key=lambda k: k == 2):
         to_chip(k).wait_recv()
         result = result + chip_in[k - 1].astype(jnp.float32)
     out_ref[...] = result.astype(jnp.bfloat16)
 
-    sends = {
-        ONE: (x < 3) | has_back,
-        TWO: (x < 2) | has_back,
-        THREE: (x < 1) | has_back,
-        FOUR: has_next,
-        FIVE: has_next & (pb > 0),
-    }
-    for kind, sent in sends.items():
+    both = KEY_CHUNKS + VALUE_CHUNKS
+    sends = (
+        (ONE, (x < 3) | has_back, both),
+        (TWO, (x < 2) | has_back, KEY_CHUNKS),
+        (TWO, (x < 3) & (pb > 0), VALUE_CHUNKS),
+        (TWO_BACK, (x == 1) & has_back, VALUE_CHUNKS),
+        (THREE, (x < 1) | has_back, both),
+        (FOUR, has_next, both),
+        (FIVE, has_next & (pb > 0), both),
+    )
+    for kind, sent, chunks in sends:
 
         @pl.when(sent)
-        def _(kind=kind):
-            for chunk in range(4):
+        def _(kind=kind, chunks=chunks):
+            for chunk in chunks:
                 message(kind, chunk).wait_send()
 
     @pl.when(has_next)
@@ -497,8 +506,8 @@
                 pltpu.VMEM((QROWS, DH), jnp.int32),
                 pltpu.VMEM((QROWS, DH), jnp.int32),
                 pltpu.VMEM((QCONV, ROWS, DH), bf16),
-                pltpu.VMEM((WINDOWS, QROWS, DH), f32),
-                pltpu.VMEM((WINDOWS * ROWS, QCONV * DH), bf16),
+                pltpu.VMEM((GROUP, WINDOWS, QROWS, DH), f32),
+                pltpu.VMEM((GROUP, WINDOWS * ROWS, QCONV * DH), bf16),
                 pltpu.VMEM((GROUP, WINDOWS, ROWS, DH), f32),
                 pltpu.VMEM((GROUP * ROWS, WINDOWS * DH), bf16),
                 pltpu.VMEM((GROUP, ROWS, DH), f32),
@@ -513,8 +522,8 @@
                 pltpu.SemaphoreType.DMA((8,)),
                 pltpu.SemaphoreType.DMA((2,)),
                 pltpu.SemaphoreType.DMA((2,)),
-                pltpu.SemaphoreType.DMA((5, 4)),
-                pltpu.SemaphoreType.DMA((5, 4)),
+                pltpu.SemaphoreType.DMA((6, 2 * CHUNKS)),
+                pltpu.SemaphoreType.DMA((6, 2 * CHUNKS)),
                 pltpu.SemaphoreType.DMA((ring_y,)),
                 pltpu.SemaphoreType.DMA((ring_y,)),
                 pltpu.SemaphoreType.DMA((far,)),

time: 40.7 us -> 35.2 us (0.86)
  the two profiles are of different devices: /device:TPU:161 before, /device:TPU:131 now
where the time goes in v3:
time: 35.2 us; the launch traced here: 35.1 us
  Pallas kernels  33.5 us (95%)
  local copies, waits for them, and re-layouts  1.57 us (4%)
    pallas_call x1, Pallas kernels, per_device(): pl.pallas_call(functools.partial(kernel, pb_size, ha_size), out_shape=jax...  33.5 us
    unnamed x1, local copies, waits for them, and re-layouts  1.57 us

profile of v3, /device:TPU:131, one launch (start us, length us, event | category | flops | bytes accessed | tf_op | source)
XLA Modules:
  0.0 35.1 jit_solution(7371423547569681939)
XLA Ops:
  0.0 33.5 %shard_map.82 = bf16[128,512]{1,0:T(8,128)(2,1)} custom-call(s32[16]{0:T(128)} %turns_hbm.1, bf16[128,512]{1,0:T(8,128)(2,1)} %q_hbm.1, bf16[128,512]{1,0:T(8,128)(2,1)} %k_hbm.1, bf16[128,512]{1,0:T(8,128)(2,1)} %v_hbm.1, f32[6,4,11]{2,1,0:T(4,128)} %bitcast.2, f32[4,4]{1,0:T(4,128)} %mix_hbm.1, f32[1,512]{1,0:T(1,128)} %bitcast.3, bf16[512,4096]{1,0:T(8,128)(2,1)} %w_hbm.1), custom_call_target="tpu_custom_call" | custom-call | tf_op jit(solution)/shard_map/pallas_call | solution.py:490
  33.5 1.6 %copy.10 = bf16[128,512]{1,0:T(8,128)(2,1)} copy(bf16[128,512]{1,0:T(8,128)(2,1)} %shard_map.82) | data formatting | bytes 262144

commit v4 on v3

--- a/solution.py
+++ b/solution.py
@@ -95,7 +95,7 @@
     def at(new_z, new_x):
         return ((new_z % ring_z) * RING_X + new_x % RING_X, ha)
 
-    x_next, x_over, x_back = at(z, x + 1), at(z, x + 2), at(z, x + RING_X - 1)
+    x_next, x_back = at(z, x + 1), at(z, x + RING_X - 1)
     z_next, z_back = at(z + 1, x), at(z + ring_z - 1, x)
     twin = (pb, y * CORES + 1 - core)
 
@@ -118,7 +118,7 @@
 
     barrier = pltpu.get_barrier_semaphore()
     has_next, has_back = z < ring_z - 1, z > 0
-    greeted = [x_next, x_over, x_back, twin]
+    greeted = [x_next, x_back, twin]
     greeted += [chip(k) for k in range(1, ring_y)]
 
     def greet(other):
@@ -164,13 +164,11 @@
         src, dst, target = {
             FOUR: (own, slot_row(4), z_next),
             ONE: (jnp.where(x < 3, own, behind), slot_row(1), x_next),
-            TWO: (jnp.where(x < 2, own, behind), slot_row(2), x_over),
+            TWO: (slot_row(1), slot_row(2), x_next),
             THREE: (jnp.where(x < 1, own, behind), slot_row(3), x_back),
             FIVE: (slot_row(1), slot_row(5), z_next),
             TWO_BACK: (slot_row(3), slot_row(2), x_back),
         }[kind]
-        if kind == TWO and chunk >= CHUNKS:
-            src, dst, target = slot_row(1), slot_row(2), x_next
         return pltpu.make_async_remote_copy(
             src_ref=win.at[pl.ds(pl.multiple_of(src + shift, 16), CHUNK)],
             dst_ref=win.at[pl.ds(dst + shift, CHUNK)],
@@ -195,8 +193,7 @@
     tail_behind = tail_copy(q_behind, qext.at[pl.ds(0, PAD)], 1, x_next)
 
     def steps(chunk):
-        two = ((TWO, 2),) if chunk < CHUNKS else ()
-        return ((ONE, 3), *two, (THREE, 1))
+        return ((ONE, 3), (THREE, 1))
 
     def from_own(chunk):
         for kind, bound in steps(chunk):
@@ -236,20 +233,20 @@
             message(THREE, chunk).wait_recv()
             message(TWO_BACK, chunk).start()
 
+    loads[2].wait()
+
+    @pl.when(has_next)
+    def _():
+        tail_z.start()
+
+    @pl.when(x < 3)
+    def _():
+        tail_own.start()
+
     loads[0].wait()
     for chunk in KEY_CHUNKS:
         to_four(chunk)
         from_own(chunk)
-    loads[2].wait()
-
-    @pl.when(has_next)
-    def _():
-        tail_z.start()
-
-    @pl.when(x < 3)
-    def _():
-        tail_own.start()
-
     loads[1].wait()
     for chunk in VALUE_CHUNKS:
         to_four(chunk)
@@ -276,16 +273,17 @@
     taps[:, 0:GROUP, 0 : REACH + 1] = scaled_theta[:, :, REACH:]
     taps[:, 0:GROUP, DH - REACH : DH] = scaled_theta[:, :, :REACH]
 
+    @pl.when(has_back)
+    def _():
+        tail_z.wait_recv()
+
+    @pl.when((x == 3) & has_back)
+    def _():
+        tail_behind.start()
+
     for chunk in KEY_CHUNKS:
         from_behind(chunk)
 
-    @pl.when(has_back)
-    def _():
-        tail_z.wait_recv()
-
-    @pl.when((x == 3) & has_back)
-    def _():
-        tail_behind.start()
 
     for chunk in VALUE_CHUNKS:
         from_own(chunk)
@@ -300,6 +298,9 @@
     lax.fori_loop(0, GROUP, make_band, 0)
     for chunk in KEY_CHUNKS:
         to_five(chunk)
+        to_two(chunk)
+    for chunk in KEY_CHUNKS:
+        back_to_two(chunk)
 
     @pl.when(pb >= 1)
     def _():
@@ -346,7 +347,11 @@
     for chunk in VALUE_CHUNKS:
         from_behind(chunk)
     for chunk in KEY_CHUNKS:
-        arrived(THREE, chunk)
+
+        @pl.when((pb >= 3) & (x != 1))
+        def _(chunk=chunk):
+            message(THREE, chunk).wait_recv()
+
     convolve(PHASES[0])
     for chunk in VALUE_CHUNKS:
         to_five(chunk)
@@ -450,9 +455,8 @@
     both = KEY_CHUNKS + VALUE_CHUNKS
     sends = (
         (ONE, (x < 3) | has_back, both),
-        (TWO, (x < 2) | has_back, KEY_CHUNKS),
-        (TWO, (x < 3) & (pb > 0), VALUE_CHUNKS),
-        (TWO_BACK, (x == 1) & has_back, VALUE_CHUNKS),
+        (TWO, (x < 3) & (pb > 0), both),
+        (TWO_BACK, (x == 1) & has_back, both),
         (THREE, (x < 1) | has_back, both),
         (FOUR, has_next, both),
         (FIVE, has_next & (pb > 0), both),

time: 35.2 us -> 34.7 us (0.986)
  the two profiles are of different devices: /device:TPU:131 before, /device:TPU:129 now
where the time goes in v4:
time: 34.7 us; the launch traced here: 34.6 us
  Pallas kernels  33.1 us (95%)
  local copies, waits for them, and re-layouts  1.57 us (5%)
    pallas_call x1, Pallas kernels, per_device(): pl.pallas_call(functools.partial(kernel, pb_size, ha_size), out_shape=jax...  33.1 us
    unnamed x1, local copies, waits for them, and re-layouts  1.57 us

profile of v4, /device:TPU:129, one launch (start us, length us, event | category | flops | bytes accessed | tf_op | source)
XLA Modules:
  0.0 34.6 jit_solution(4238926839999154318)
XLA Ops:
  0.0 33.1 %shard_map.82 = bf16[128,512]{1,0:T(8,128)(2,1)} custom-call(s32[16]{0:T(128)} %turns_hbm.1, bf16[128,512]{1,0:T(8,128)(2,1)} %q_hbm.1, bf16[128,512]{1,0:T(8,128)(2,1)} %k_hbm.1, bf16[128,512]{1,0:T(8,128)(2,1)} %v_hbm.1, f32[6,4,11]{2,1,0:T(4,128)} %bitcast.2, f32[4,4]{1,0:T(4,128)} %mix_hbm.1, f32[1,512]{1,0:T(1,128)} %bitcast.3, bf16[512,4096]{1,0:T(8,128)(2,1)} %w_hbm.1), custom_call_target="tpu_custom_call" | custom-call | tf_op jit(solution)/shard_map/pallas_call | solution.py:494
  33.1 1.6 %copy.10 = bf16[128,512]{1,0:T(8,128)(2,1)} copy(bf16[128,512]{1,0:T(8,128)(2,1)} %shard_map.82) | data formatting | bytes 262144

commit v5 on v4

--- a/solution.py
+++ b/solution.py
@@ -25,7 +25,7 @@
 QROWS = PAD + ROWS
 MESH = pl.DeviceIdType.MESH
 FOUR, ONE, TWO, THREE, FIVE, TWO_BACK = range(6)
-PHASES = ((6, 5, 2), (4, 3), (0, 1))
+PHASES = ((6, 5, 2, 4, 3), (0, 1))
 FAR = 2
 CHUNKS = 4
 CHUNK = ROWS // CHUNKS
@@ -352,7 +352,6 @@
         def _(chunk=chunk):
             message(THREE, chunk).wait_recv()
 
-    convolve(PHASES[0])
     for chunk in VALUE_CHUNKS:
         to_five(chunk)
         to_two(chunk)
@@ -360,11 +359,11 @@
         back_to_two(chunk)
     for chunk in KEY_CHUNKS:
         arrived(TWO, chunk)
+    convolve(PHASES[0])
+    for chunk in KEY_CHUNKS:
+        arrived(FIVE, chunk)
+
     convolve(PHASES[1])
-    for chunk in KEY_CHUNKS:
-        arrived(FIVE, chunk)
-
-    convolve(PHASES[2])
     for h in range(GROUP):
         peak = conv_buf[h, 0]
         for t in range(1, WINDOWS):
@@ -433,7 +432,7 @@
             device_id_type=MESH,
         )
 
-    order = [2, 1, 3, 0] if ring_y == 4 else list(range(ring_y - 1, -1, -1))
+    order = [1, 3, 2, 0] if ring_y == 4 else list(range(ring_y - 1, -1, -1))
     for k in order:
         core_out[k] = partial(k, 1 - core).astype(jnp.bfloat16)
         to_twin(k).start()

time: 34.7 us -> 34.4 us (level)
  the two profiles are of different devices: /device:TPU:129 before, /device:TPU:128 now
where the time goes in v5:
time: 34.4 us; the launch traced here: 34.3 us
  Pallas kernels  32.8 us (95%)
  local copies, waits for them, and re-layouts  1.57 us (5%)
    pallas_call x1, Pallas kernels, per_device(): pl.pallas_call(functools.partial(kernel, pb_size, ha_size), out_shape=jax...  32.8 us
    unnamed x1, local copies, waits for them, and re-layouts  1.57 us

profile of v5, /device:TPU:128, one launch (start us, length us, event | category | flops | bytes accessed | tf_op | source)
XLA Modules:
  0.0 34.3 jit_solution(1965775662302680270)
XLA Ops:
  0.0 32.8 %shard_map.82 = bf16[128,512]{1,0:T(8,128)(2,1)} custom-call(s32[16]{0:T(128)} %turns_hbm.1, bf16[128,512]{1,0:T(8,128)(2,1)} %q_hbm.1, bf16[128,512]{1,0:T(8,128)(2,1)} %k_hbm.1, bf16[128,512]{1,0:T(8,128)(2,1)} %v_hbm.1, f32[6,4,11]{2,1,0:T(4,128)} %bitcast.2, f32[4,4]{1,0:T(4,128)} %mix_hbm.1, f32[1,512]{1,0:T(1,128)} %bitcast.3, bf16[512,4096]{1,0:T(8,128)(2,1)} %w_hbm.1), custom_call_target="tpu_custom_call" | custom-call | tf_op jit(solution)/shard_map/pallas_call | solution.py:493
  32.8 1.6 %copy.10 = bf16[128,512]{1,0:T(8,128)(2,1)} copy(bf16[128,512]{1,0:T(8,128)(2,1)} %shard_map.82) | data formatting | bytes 262144
